TPU v7x, 512 devices: a whole 4x4x16 slice. The times are simulated.
512 devices in a mesh: vox: 64 (over z, x_hi, core), tm: 4 (over y), mod: 2 (over x_lo).
Axes of the slice: x: 4 (x_hi: 2, x_lo: 2; x = x_hi * 2 + x_lo), y: 4, z: 16, core: 2. Of those that a mesh axis runs over, the one named last changes fastest.
Arguments:
- scans: bfloat16 [2, 16384, 48, 512], P('mod', 'vox', None, 'tm'), may hold values from -6 to 6
- spatial_init: float32 [2, 16384, 128], P('mod', 'vox'), may hold values from -6 to 6
- time_init: float32 [512, 128], P('tm'), may hold values from -0.09375 to 0.09375
- subject_init: float32 [48, 128], replicated, may hold values from -6 to 6
- hrf_kernel: float32 [16], replicated, may hold values from 0.05 to 0.5
- kept_blocks: int32 [48, 32], P(None, 'tm'), may hold values 0 or 1
Outputs:
- spatial_factors: float32 [2, 16384, 128], P('mod', 'vox')
- time_factors: float32 [512, 128], P('tm')
- subject_factors: float32 [48, 128], replicated
All inputs are finite; a program needn't handle non-finite values. No bound on the sum of `kept_blocks` on one device may be relied on, other than what follows from the above.
Results may differ from a plain program's by a relative error of at most 0.003.
Values sent between devices are 32-bit elements; how exact they have to be, the bound alone decides.
A program may use at most 64 MiB of HBM per device.

v0:
```python
import jax
import jax.numpy as jnp
from jax import lax
from jax.sharding import PartitionSpec as P

RIDGE = 0.1
EPS = 1e-06


def shifted(block, axis, distance):
    devices = range(lax.axis_size(axis))
    route = [(i - distance, i) for i in devices if i - distance in devices]
    return lax.ppermute(block, axis, route)


def ridge_solve(right_side, gram):
    eye_mat = jnp.eye(gram.shape[0], dtype=gram.dtype)
    factor = jnp.linalg.cholesky(gram + RIDGE * eye_mat)
    return jax.scipy.linalg.cho_solve((factor, True), right_side.T).T


def hgram(left, right):
    return jnp.dot(left.T, right, precision=lax.Precision.HIGHEST)


def conv_causal(series, kernel):
    reach = kernel.shape[0]
    count = series.shape[0]
    tail_part = series[count - (reach - 1) :]
    before = shifted(tail_part, "tm", 1)
    padded = jnp.concatenate([before, series])
    summed = jnp.zeros_like(series)
    for lag in range(reach):
        summed = summed + kernel[lag] * padded[reach - 1 - lag : reach - 1 - lag + count]
    return summed


def conv_adjoint(series, kernel):
    reach = kernel.shape[0]
    count = series.shape[0]
    head_part = series[: reach - 1]
    after = shifted(head_part, "tm", -1)
    padded = jnp.concatenate([series, after])
    summed = jnp.zeros_like(series)
    for lag in range(reach):
        summed = summed + kernel[lag] * padded[lag : lag + count]
    return summed


def per_device(scans, spatial_init, time_init, subject_init, hrf_kernel, kept_blocks):
    is_fmri = lax.axis_index("mod") == 0
    row_count, subj_count, tr_count = (scans.shape[1], scans.shape[2], scans.shape[3])
    rank_count = subject_init.shape[1]
    total_rows = row_count * lax.axis_size("vox")
    total_trs = tr_count * lax.axis_size("tm")
    factor_t = jnp.where(is_fmri, conv_causal(time_init, hrf_kernel), time_init)
    block_len = tr_count // kept_blocks.shape[1]
    kept_tr = jnp.logical_or(
        jnp.repeat(kept_blocks, block_len, axis=1) > 0, jnp.logical_not(is_fmri)
    )
    khatri = (
        (subject_init[:, None, :] * factor_t[None, :, :])
        .astype(jnp.bfloat16)
        .reshape(subj_count * tr_count, rank_count)
    )
    signal = scans[0].reshape(row_count, subj_count * tr_count)
    previous = spatial_init[0].astype(jnp.bfloat16)
    modeled = lax.dot_general(
        previous, khatri, (((1,), (1,)), ((), ())), preferred_element_type=jnp.float32
    )
    filled = jnp.where(
        kept_tr.reshape(1, subj_count * tr_count), signal.astype(jnp.float32), modeled
    ).astype(jnp.bfloat16)
    mttkrp_part = jnp.dot(filled, khatri, preferred_element_type=jnp.float32)
    tgram_part = hgram(factor_t, factor_t)
    mttkrp, time_gram = lax.psum((mttkrp_part, tgram_part), "tm")
    subj_gram = hgram(subject_init, subject_init)
    updated = ridge_solve(mttkrp, subj_gram * time_gram)
    rgram_part = hgram(updated, updated)
    khatri2 = (
        (updated[:, None, :] * subject_init[None, :, :])
        .astype(jnp.bfloat16)
        .reshape(row_count * subj_count, rank_count)
    )
    proj = lax.dot_general(
        filled.reshape(row_count * subj_count, tr_count),
        khatri2,
        (((0,), (0,)), ((), ())),
        preferred_element_type=jnp.float32,
    )
    adjoint = jnp.where(is_fmri, conv_adjoint(proj, hrf_kernel), proj)
    tgram_terms = rgram_part * subj_gram
    time_rhs, gram_t = lax.psum((adjoint, tgram_terms), ("vox", "mod"))
    raw = total_rows * ridge_solve(time_rhs, gram_t)
    sumsq = lax.psum(jnp.sum(raw * raw, axis=0), "tm")
    time_factors = raw / jnp.sqrt(sumsq / total_trs + EPS)
    scale_c = (2.0 * total_rows * total_trs) ** (-0.5)
    scaled_eeg = time_factors * scale_c
    scaled_t = jnp.where(is_fmri, conv_causal(scaled_eeg, hrf_kernel), scaled_eeg)
    khatri3 = (updated[:, None, :] * scaled_t[None, :, :]).astype(jnp.bfloat16)
    subj_part = lax.dot_general(
        filled.reshape(row_count, subj_count, tr_count),
        khatri3,
        (((0, 2), (0, 1)), ((), ())),
        preferred_element_type=jnp.float32,
    )
    sgram_part = hgram(scaled_t, scaled_t)
    row_gram = lax.psum(rgram_part, "vox")
    scaled_gram = lax.psum(sgram_part, "tm")
    leading = jnp.logical_and(lax.axis_index("vox") == 0, lax.axis_index("tm") == 0)
    gram_term = jnp.where(leading, row_gram * scaled_gram, 0.0)
    subject_rhs, gram_c = lax.psum((subj_part, gram_term), ("vox", "tm", "mod"))
    subject_factors = ridge_solve(subject_rhs, gram_c)
    return (updated[None], time_factors, subject_factors)


def solution(mesh):
    return jax.shard_map(
        per_device,
        mesh=mesh,
        in_specs=(
            P("mod", "vox", None, "tm"),
            P("mod", "vox", None),
            P("tm", None),
            P(),
            P(),
            P(None, "tm"),
        ),
        out_specs=(P("mod", "vox", None), P("tm", None), P()),
        check_vma=False,
    )
```

profile of v0, /device:TPU:1, one launch (start us, length us, event | category | flops | bytes accessed | tf_op | source)
XLA Modules:
  0.0 1485.5 jit_solution(1407539403140570844)
XLA Ops:
  7.9 4.0 collective-permute-start
  14.6 5.1 copy.23
  20.1 10.2 fusion.98
  31.6 4.8 fusion.4
  38.4 3.1 copy.26
  41.5 5.7 reshape.87
  47.2 50.4 %all-reduce.16.cloned.1.call-done = (f32[256,128]{1,0:T(8,128)}, f32[128,128]{1,0:T(8,128)}) async-done(((f32[256,128]{1,0:T(8,128)}, f32[128,128]{1,0:T(8,128)}), (f32[256,128]{1,0:T(8,128)}, f32[128,128]{1,0:T(8,128)})) %all-reduce.16.cloned.1.call-update) | async-done | bytes 196624 | tf_op jit(solution)/shard_map/psum | solution.py:76
  99.0 11.7 cholesky.59
  112.0 9.8 custom-call.23
  128.6 2.2 collective-permute-done.1
  130.8 10.8 fusion.54
  141.9 322.2 %all-reduce.14.cloned.1.call-done = (f32[128,128]{1,0:T(8,128)}, f32[128,128]{1,0:T(8,128)}) async-done(((f32[128,128]{1,0:T(8,128)}, f32[128,128]{1,0:T(8,128)}), (f32[128,128]{1,0:T(8,128)}, f32[128,128]{1,0:T(8,128)})) %all-reduce.14.cloned.1.call-update) | async-done | bytes 131088 | tf_op jit(solution)/shard_map/psum | solution.py:93
  466.6 12.5 cholesky.70
  481.1 10.6 custom-call.24
  493.2 8.5 psum.67
  504.4 10.4 fusion.10
  515.7 3.5 copy.32
  519.9 429.4 %all-reduce.8.cloned.1.call-done = f32[128,128]{1,0:T(8,128)} async-done(((f32[128,128]{1,0:T(8,128)}), f32[128,128]{1,0:T(8,128)}) %all-reduce.8.cloned.1.call-update) | async-done | bytes 65552 | tf_op jit(solution)/shard_map/psum | solution.py:108
  949.3 54.3 %all-reduce.10.cloned.1.call-done = f32[128,128]{1,0:T(8,128)} async-done(((f32[128,128]{1,0:T(8,128)}), f32[128,128]{1,0:T(8,128)}) %all-reduce.10.cloned.1.call-update) | async-done | bytes 65552 | tf_op jit(solution)/shard_map/psum | solution.py:109
  1005.2 3.2 fusion.5
  1008.4 106.8 %psum.71 = f32[48,128]{1,0:T(8,128)S(1)} all-reduce(f32[48,128]{1,0:T(8,128)S(1)} %fusion.5), channel_id=1, replica_groups=mesh['vox'=64,'tm'=4,'mod'=2] {'vox','tm','mod'}, use_global_device_ids=true, to_apply=%region_11.13 | all-reduce | flops 6144 | bytes 49152 | tf_op jit(solution)/shard_map/psum | solution.py:112
  1115.1 337.9 %all-reduce.12.cloned.1.call-done = f32[128,128]{1,0:T(8,128)} async-done(((f32[128,128]{1,0:T(8,128)}), f32[128,128]{1,0:T(8,128)}) %all-reduce.12.cloned.1.call-update) | async-done | bytes 65552 | tf_op jit(solution)/shard_map/psum | solution.py:112
  1455.0 11.7 cholesky.81
  1468.0 9.8 custom-call.25
  (69 shorter events, 32.2 us)
Async XLA Ops:
  7.2 90.5 %all-reduce.16.cloned.1.call-start = ((), (), s32[]{:S(2)}) async-start(), calls=%async_computation.4 | async-start | bytes 393216 | tf_op jit(solution)/shard_map/psum | solution.py:76
  7.9 12.2 collective-permute-start
  14.6 5.5 copy-start.3
  14.6 16.6 %copy-start.1 = (f32[48,128]{1,0:T(8,128)S(1)}, f32[48,128]{1,0:T(8,128)}, u32[]{:S(2)}) copy-start(f32[48,128]{1,0:T(8,128)} %param.10) | copy-start | bytes 73732
  14.6 17.0 %copy-start.2 = (f32[1,256,128]{2,1,0:T(8,128)S(1)}, f32[1,256,128]{2,1,0:T(8,128)}, u32[]{:S(2)}) copy-start(f32[1,256,128]{2,1,0:T(8,128)} %param.8) | copy-start | bytes 393220
  38.1 425.9 %all-reduce.14.cloned.1.call-start = ((), (), s32[]{:S(2)}) async-start(), calls=%async_computation.3 | async-start | bytes 262144 | tf_op jit(solution)/shard_map/psum | solution.py:93
  123.4 1.9 copy-start
  126.4 4.4 collective-permute-start.1
  141.6 807.7 %all-reduce.8.cloned.1.call-start = ((), (), s32[]{:S(2)}) async-start(), calls=%async_computation | async-start | bytes 131072 | tf_op jit(solution)/shard_map/psum | solution.py:108
  502.3 2.1 collective-permute-start.2
  504.3 499.4 %all-reduce.10.cloned.1.call-start = ((), (), s32[]{:S(2)}) async-start(), calls=%async_computation.1 | async-start | bytes 131072 | tf_op jit(solution)/shard_map/psum | solution.py:109
  515.7 937.4 %all-reduce.12.cloned.1.call-start = ((), (), s32[]{:S(2)}) async-start(), calls=%async_computation.2 | async-start | bytes 131072 | tf_op jit(solution)/shard_map/psum | solution.py:112
Sparse Core Ops, SparseCore 0:
  38.3 59.3 all-reduce.15
  141.7 322.2 all-reduce.13
  504.4 444.8 all-reduce.7
  951.5 52.1 all-reduce.9
  1009.8 443.1 all-reduce.11
where the time goes:
time: 1490 us
  waiting for transfers between devices  1200 us (81%)
  blocking collectives  115 us (8%)
  other arithmetic  109 us (7%)
  local copies, waits for them, and re-layouts  23.8 us (2%)
  matrix products  18.6 us (1%)
    psum x1, waiting for transfers between devices, per_device(): row_gram = lax.psum(rgram_part, 'vox')  429 us
    psum x1, waiting for transfers between devices, per_device(): subject_rhs, gram_c = lax.psum((subj_part, gram_term), ('vox', 'tm', 'mod'))  338 us
    psum x1, waiting for transfers between devices, per_device(): time_rhs, gram_t = lax.psum((adjoint, tgram_terms), ('vox', 'mod'))  322 us
    psum x1, blocking collectives, per_device(): subject_rhs, gram_c = lax.psum((subj_part, gram_term), ('vox', 'tm', 'mod'))  107 us
    psum x1, waiting for transfers between devices, per_device(): scaled_gram = lax.psum(sgram_part, 'tm')  54.3 us
    psum x1, waiting for transfers between devices, per_device(): mttkrp, time_gram = lax.psum((mttkrp_part, tgram_part), 'tm')  50.4 us
    another operation x9, other arithmetic, ridge_solve(): factor = jnp.linalg.cholesky(gram + RIDGE * eye_mat)  38 us
    another operation x6, other arithmetic, ridge_solve(): return jax.scipy.linalg.cho_solve((factor, True), right_side.T).T  32.9 us
  transfers between devices with their start and end apart: 8, of which 7 were waited for; matrix products, arithmetic and copies ran while one was open for 2% of the time, Pallas kernels for 0%

commit v1 on v0

--- a/solution.py
+++ b/solution.py
@@ -5,6 +5,12 @@
 
 RIDGE = 0.1
 EPS = 1e-06
+
+
+def gather_and_add(value, axis):
+    parts = lax.all_gather(value, axis, axis=0, tiled=False)
+    summed = parts.sum(axis=0)
+    return summed
 
 
 def shifted(block, axis, distance):
@@ -105,7 +111,7 @@
         preferred_element_type=jnp.float32,
     )
     sgram_part = hgram(scaled_t, scaled_t)
-    row_gram = lax.psum(rgram_part, "vox")
+    row_gram = gather_and_add(rgram_part, "vox")
     scaled_gram = lax.psum(sgram_part, "tm")
     leading = jnp.logical_and(lax.axis_index("vox") == 0, lax.axis_index("tm") == 0)
     gram_term = jnp.where(leading, row_gram * scaled_gram, 0.0)

time: 1490 us -> 1150 us (0.77)
  waiting for transfers between devices: 1200 us -> 854 us
    psum x1 -> x0, waiting for transfers between devices: 429 us -> none  [per_device(): row_gram = lax.psum(rgram_part, 'vox')]
    all_gather x0 -> x1, waiting for transfers between devices: none -> 91.9 us  [gather_and_add(): parts = lax.all_gather(value, axis, axis=0, tiled=False)]
  transfers between devices with their start and end apart: 8 -> 8, of which waited for: 7 -> 7; matrix products, arithmetic and copies ran while one was open for 2% -> 6% of each run, Pallas kernels for 0% -> 0%
where the time goes in v1:
time: 1150 us; the launch traced here: 1140 us
  waiting for transfers between devices  854 us (74%)
  blocking collectives  116 us (10%)
  other arithmetic  112 us (10%)
  local copies, waits for them, and re-layouts  23.7 us (2%)
  matrix products  16.7 us (1%)
  between operations  14.8 us (1%)
    psum x1, waiting for transfers between devices, per_device(): subject_rhs, gram_c = lax.psum((subj_part, gram_term), ('vox', 'tm', 'mod'))  339 us
    psum x1, waiting for transfers between devices, per_device(): time_rhs, gram_t = lax.psum((adjoint, tgram_terms), ('vox', 'mod'))  321 us
    psum x1, blocking collectives, per_device(): subject_rhs, gram_c = lax.psum((subj_part, gram_term), ('vox', 'tm', 'mod'))  107 us
    all_gather x1, waiting for transfers between devices, gather_and_add(): parts = lax.all_gather(value, axis, axis=0, tiled=False)  91.9 us
    psum x1, waiting for transfers between devices, per_device(): mttkrp, time_gram = lax.psum((mttkrp_part, tgram_part), 'tm')  50.4 us
    psum x1, waiting for transfers between devices, per_device(): scaled_gram = lax.psum(sgram_part, 'tm')  48.2 us
    another operation x9, other arithmetic, ridge_solve(): factor = jnp.linalg.cholesky(gram + RIDGE * eye_mat)  38 us
    another operation x6, other arithmetic, ridge_solve(): return jax.scipy.linalg.cho_solve((factor, True), right_side.T).T  32.9 us
  transfers between devices with their start and end apart: 8, of which 7 were waited for; matrix products, arithmetic and copies ran while one was open for 6% of the time, Pallas kernels for 0%

profile of v1, /device:TPU:1, one launch (start us, length us, event | category | flops | bytes accessed | tf_op | source)
XLA Modules:
  0.0 1143.6 jit_solution(12530694061414593140)
XLA Ops:
  7.9 4.0 collective-permute-start
  14.6 5.1 copy.23
  20.1 10.2 fusion.98
  31.6 4.8 fusion.4
  38.4 3.1 copy.26
  41.5 5.7 reshape.87
  47.2 50.4 %all-reduce.13.cloned.1.call-done = (f32[256,128]{1,0:T(8,128)}, f32[128,128]{1,0:T(8,128)}) async-done(((f32[256,128]{1,0:T(8,128)}, f32[128,128]{1,0:T(8,128)}), (f32[256,128]{1,0:T(8,128)}, f32[128,128]{1,0:T(8,128)})) %all-reduce.13.cloned.1.call-update) | async-done | bytes 196624 | tf_op jit(solution)/shard_map/psum | solution.py:82
  99.0 11.7 %cholesky.59 = f32[128,128]{1,0:T(8,128)S(1)} custom-call(f32[128,128]{1,0:T(8,128)S(1)} %copy.21), custom_call_target="Cholesky" | custom-call | tf_op jit(solution)/shard_map/jit(cholesky)/cholesky | solution.py:24
  112.0 9.8 custom-call.23
  128.6 2.2 collective-permute-done.1
  130.8 10.8 fusion.54
  142.6 321.4 %all-reduce.11.cloned.1.call-done = (f32[128,128]{1,0:T(8,128)}, f32[128,128]{1,0:T(8,128)}) async-done(((f32[128,128]{1,0:T(8,128)}, f32[128,128]{1,0:T(8,128)}), (f32[128,128]{1,0:T(8,128)}, f32[128,128]{1,0:T(8,128)})) %all-reduce.11.cloned.1.call-update) | async-done | bytes 131088 | tf_op jit(solution)/shard_map/psum | solution.py:99
  466.6 12.5 %cholesky.70 = f32[128,128]{1,0:T(8,128)S(1)} custom-call(f32[128,128]{1,0:T(8,128)} %copy.25), custom_call_target="Cholesky" | custom-call | tf_op jit(solution)/shard_map/jit(cholesky)/cholesky | solution.py:24
  481.1 10.7 custom-call.24
  493.2 8.9 psum.60
  504.9 10.4 fusion.10
  516.3 3.4 copy.32
  520.5 91.9 %all-gather.3.cloned.1.call-done = f32[8192,128]{1,0:T(8,128)} async-done(((f32[128,128]{1,0:T(8,128)}), f32[8192,128]{1,0:T(8,128)}) %all-gather.3.cloned.1.call-update) | async-done | bytes 4194320 | tf_op jit(solution)/shard_map/all_gather | solution.py:11
  612.4 2.4 reduce_sum.19
  614.8 48.2 %all-reduce.7.cloned.1.call-done = f32[128,128]{1,0:T(8,128)} async-done(((f32[128,128]{1,0:T(8,128)}), f32[128,128]{1,0:T(8,128)}) %all-reduce.7.cloned.1.call-update) | async-done | bytes 65552 | tf_op jit(solution)/shard_map/psum | solution.py:115
  665.8 106.7 %psum.63 = f32[48,128]{1,0:T(8,128)S(1)} all-reduce(f32[48,128]{1,0:T(8,128)S(1)} %fusion.5), channel_id=1, replica_groups=mesh['vox'=64,'tm'=4,'mod'=2] {'vox','tm','mod'}, use_global_device_ids=true, to_apply=%region_11.13 | all-reduce | flops 6144 | bytes 49152 | tf_op jit(solution)/shard_map/psum | solution.py:118
  772.5 338.6 %all-reduce.9.cloned.1.call-done = f32[128,128]{1,0:T(8,128)} async-done(((f32[128,128]{1,0:T(8,128)}), f32[128,128]{1,0:T(8,128)}) %all-reduce.9.cloned.1.call-update) | async-done | bytes 65552 | tf_op jit(solution)/shard_map/psum | solution.py:118
  1113.1 11.7 %cholesky.81 = f32[128,128]{1,0:T(8,128)S(1)} custom-call(f32[128,128]{1,0:T(8,128)S(1)} %copy.29), custom_call_target="Cholesky" | custom-call | tf_op jit(solution)/shard_map/jit(cholesky)/cholesky | solution.py:24
  1126.1 9.8 custom-call.25
  (72 shorter events, 34.4 us)
Async XLA Ops:
  7.2 90.5 %all-reduce.13.cloned.1.call-start = ((), (), s32[]{:S(2)}) async-start(), calls=%async_computation.4 | async-start | bytes 393216 | tf_op jit(solution)/shard_map/psum | solution.py:82
  7.9 12.2 %collective-permute-start = (f32[15,128]{1,0:T(8,128)S(1)}, f32[15,128]{1,0:T(8,128)S(1)}, u32[]{:S(2)}, u32[]{:S(2)}) collective-permute-start(f32[15,128]{1,0:T(8,128)S(1)} %slice.266), channel_id=1, source_target_pairs={{0,2},{2,4},{4,6},{1,3},{3,5},{5,7},{8,10},{10,12},{12,14},{9,11},... | collective-permute-start | bytes 23048 | tf_op jit(solution)/shard_map/ppermute | solution.py:19
  14.6 5.5 copy-start.4
  14.6 16.6 %copy-start.2 = (f32[48,128]{1,0:T(8,128)S(1)}, f32[48,128]{1,0:T(8,128)}, u32[]{:S(2)}) copy-start(f32[48,128]{1,0:T(8,128)} %param.10) | copy-start | bytes 73732
  14.6 17.0 %copy-start.3 = (f32[1,256,128]{2,1,0:T(8,128)S(1)}, f32[1,256,128]{2,1,0:T(8,128)}, u32[]{:S(2)}) copy-start(f32[1,256,128]{2,1,0:T(8,128)} %param.8) | copy-start | bytes 393220
  38.1 425.9 %all-reduce.11.cloned.1.call-start = ((), (), s32[]{:S(2)}) async-start(), calls=%async_computation.3 | async-start | bytes 262144 | tf_op jit(solution)/shard_map/psum | solution.py:99
  123.4 1.9 copy-start
  126.4 4.4 collective-permute-start.1
  141.6 470.8 %all-gather.3.cloned.1.call-start = ((), (), s32[]{:S(2)}) async-start(), calls=%async_computation.2 | async-start | bytes 4259840 | tf_op jit(solution)/shard_map/all_gather | solution.py:11
  142.3 520.6 %all-reduce.7.cloned.1.call-start = ((), (), s32[]{:S(2)}) async-start(), calls=%async_computation | async-start | bytes 131072 | tf_op jit(solution)/shard_map/psum | solution.py:115
  502.7 2.2 collective-permute-start.2
  516.2 594.9 %all-reduce.9.cloned.1.call-start = ((), (), s32[]{:S(2)}) async-start(), calls=%async_computation.1 | async-start | bytes 131072 | tf_op jit(solution)/shard_map/psum | solution.py:118
  519.7 144.8 %copy-start.1 = (bf16[256,48,128]{2,1,0:T(8,128)(2,1)S(1)}, bf16[256,48,128]{2,1,0:T(8,128)(2,1)}, u32[]{:S(2)}) copy-start(bf16[256,48,128]{2,1,0:T(8,128)(2,1)} %copy.32) | copy-start | bytes 9437188
Sparse Core Ops, SparseCore 0:
  38.3 59.3 all-reduce.12
  141.7 322.2 all-reduce.10
  467.8 144.4 all-gather.2
  614.6 48.3 all-reduce.6
  668.3 442.8 all-reduce.8
